TPU v7x, 128 devices: a whole 4x4x4 slice. The times are simulated.
128 devices in a mesh: lat: 8 (over z, core), ord: 16 (over x, y).
Axes of the slice: x: 4, y: 4, z: 4, core: 2. Of those that a mesh axis runs over, the one named last changes fastest.
Arguments:
- grid_field: float32 [1440, 768], P('ord', 'lat'), may hold values from -6 to 6
- legendre: bfloat16 [768, 720, 720], P('lat', 'ord'), may hold values from -0.21875 to 0.21875
- cycle_weight: float32 [768], P('lat'), may hold values from 0.2 to 2.4
- slot_order: int32 [720], replicated, may hold values from 0 to 719, each once
- kappa: float32 [8, 720], replicated, may hold values from 0.1 to 1
- eta: float32 [4, 2, 720], replicated, may hold values from -1 to 1
- pairs: int32 [2, 2], replicated, may hold values from 0 to 7
- target: float32 [2, 4], replicated, may hold values from -1 to 1
Outputs:
- gradient: float32 [1440, 768], P('ord', 'lat')
Inputs may be any that keep to these rules, and one draw needn't show every extreme that they name: `slot_order`: a permutation of the orders.
All inputs are finite; a program needn't handle non-finite values.
Results may differ from a plain program's by a relative error of at most 0.0003.
Values sent between devices are 32-bit elements; how exact they have to be, the bound alone decides.
No kernel may reach another device: no remote copies, remote signals or barrier semaphores. Data moves between devices by JAX's collectives and lax.ppermute only.
A program may use at most 128 MiB of HBM per device.

v0:
```python
import math

import jax
import jax.numpy as jnp
from jax import lax
from jax.sharding import PartitionSpec as P

HIGHEST_PREC = lax.Precision.HIGHEST
MOD_EPSILON = 0.01


def shards(grid_field, legendre, cycle_weight, slot_order, kappa, eta, pairs, target):
    lat_count = lax.axis_size("lat")
    ord_count = lax.axis_size("ord")
    phi_dev, cycle_dev = grid_field.shape
    slot_dev = legendre.shape[1]
    degrees = legendre.shape[2]
    nphi = phi_dev * ord_count
    ntheta = cycle_dev * lat_count
    degree_dev = degrees // lat_count
    pair_count, dir_count = target.shape
    combos = pair_count * dir_count
    norming = math.sqrt(2.0 / nphi)
    my_slots = lax.dynamic_slice_in_dim(slot_order, lax.axis_index("ord") * slot_dev, slot_dev, 0)
    degree_ids = jnp.arange(degrees, dtype=jnp.int32)
    legendre_rows = jnp.where(
        degree_ids[None, None, :] >= my_slots[None, :, None], legendre.astype(jnp.float32), 0.0
    )
    phase = slot_order[:, None] * jnp.arange(nphi, dtype=jnp.int32)[None, :] % nphi
    angles = phase.astype(jnp.float32) * (2.0 * math.pi / nphi)
    harmonics = jnp.stack([jnp.cos(angles), jnp.sin(angles)])
    selector = (my_slots[:, None] == degree_ids[None, :]).astype(jnp.float32)
    eta_local = jnp.einsum("drl,sl->drs", eta, selector, precision=HIGHEST_PREC)
    scale_ids = jnp.arange(kappa.shape[0], dtype=jnp.int32)
    pick_first = (pairs[:, 0:1] == scale_ids[None, :]).astype(jnp.float32)
    pick_second = (pairs[:, 1:2] == scale_ids[None, :]).astype(jnp.float32)
    kap_first = jnp.dot(pick_first, kappa, precision=HIGHEST_PREC)
    kap_second = jnp.dot(pick_second, kappa, precision=HIGHEST_PREC)

    def longitude_forward(segment):
        spectra = norming * jnp.einsum("qsk,bkr->bqsr", harmonics, segment, precision=HIGHEST_PREC)
        return lax.all_to_all(spectra, "ord", split_axis=2, concat_axis=3, tiled=True)

    def grid_to_cycles(fields):
        return longitude_forward(
            lax.all_to_all(fields, "ord", split_axis=2, concat_axis=1, tiled=True)
        )

    def longitude_inverse(segment):
        values = norming * jnp.einsum("qsk,bqsr->bkr", harmonics, segment, precision=HIGHEST_PREC)
        return lax.all_to_all(values, "ord", split_axis=1, concat_axis=2, tiled=True)

    def cycles_to_grid(cycles):
        return longitude_inverse(
            lax.all_to_all(cycles, "ord", split_axis=3, concat_axis=2, tiled=True)
        )

    def harmonic_partials(cycles, weighted):
        source = cycles * cycle_weight if weighted else cycles
        return jnp.einsum("rsl,bqsr->lbqs", legendre_rows, source, precision=HIGHEST_PREC)

    def reduce_degrees(cycles, weighted, mixer):
        partials = lax.psum_scatter(
            harmonic_partials(cycles, weighted), "lat", scatter_dimension=0, tiled=True
        )
        return mixer(partials, lax.axis_index("lat") * degree_dev, degree_dev)

    def to_grid(coeffs, expand, weighted):
        segment = lax.all_gather(coeffs, "lat", axis=0, tiled=True)
        expanded = expand(segment, jnp.int32(0))
        cycles = jnp.einsum("rsl,lbqs->bqsr", legendre_rows, expanded, precision=HIGHEST_PREC)
        if weighted:
            cycles = cycles * cycle_weight
        return cycles_to_grid(cycles)

    def keep_same(partials, offset, amount):
        return partials

    def expand_plain(segment, offset):
        return segment

    def expand_first(segment, offset):
        row_count = segment.shape[0]
        both_rows = jnp.stack([kap_first, kap_second])
        expanded = jnp.einsum(
            "wpl,drs,lqs->lwpdrqs", both_rows, eta_local, segment[:, 0], precision=HIGHEST_PREC
        )
        return expanded.reshape(row_count, 4 * combos, 2, slot_dev)

    def expand_second(segment, offset):
        row_count = segment.shape[0]
        viewed = segment.reshape(row_count, pair_count, dir_count, 2, slot_dev)
        expanded = jnp.einsum(
            "pl,drs,lpdqs->lpdrqs", kap_second, eta_local, viewed, precision=HIGHEST_PREC
        )
        return expanded.reshape(row_count, 2 * combos, 2, slot_dev)

    def filter_sum(partials, kap_rows, keep_pairs):
        row_count = partials.shape[0]
        viewed = partials.reshape(row_count, pair_count, dir_count, 2, 2, slot_dev)
        if keep_pairs:
            mixed = jnp.einsum(
                "pl,drs,lpdrqs->lpdqs", kap_rows, eta_local, viewed, precision=HIGHEST_PREC
            )
            return mixed.reshape(row_count, combos, 2, slot_dev)
        mixed = jnp.einsum(
            "pl,drs,lpdrqs->lqs", kap_rows, eta_local, viewed, precision=HIGHEST_PREC
        )
        return mixed[:, None]

    def mix_backward_first(partials, offset, amount):
        kap_rows = lax.dynamic_slice_in_dim(kap_second, offset, amount, 1)
        upper = filter_sum(partials[:, : 2 * combos], kap_rows, True)
        lower = filter_sum(partials[:, 2 * combos :], kap_rows, False)
        return jnp.concatenate([upper, lower], axis=1)

    def mix_backward_second(partials, offset, amount):
        kap_rows = lax.dynamic_slice_in_dim(kap_first, offset, amount, 1)
        return filter_sum(partials, kap_rows, False)

    base = reduce_degrees(grid_to_cycles(grid_field[None]), True, keep_same)
    wavelet_maps = to_grid(base, expand_first, False)
    wavelet_maps = wavelet_maps.reshape(2, pair_count, dir_count, 2, phi_dev, cycle_dev)
    first_maps = wavelet_maps[0]
    pair_maps = wavelet_maps[1]
    first_mod = jnp.sqrt(first_maps[:, :, 0] ** 2 + first_maps[:, :, 1] ** 2 + MOD_EPSILON)
    pair_mod = jnp.sqrt(pair_maps[:, :, 0] ** 2 + pair_maps[:, :, 1] ** 2 + MOD_EPSILON)
    mod_coef = reduce_degrees(
        grid_to_cycles(first_mod.reshape(combos, phi_dev, cycle_dev)), True, keep_same
    )
    second_maps = to_grid(mod_coef, expand_second, False)
    second_maps = second_maps.reshape(pair_count, dir_count, 2, phi_dev, cycle_dev)
    second_mod = jnp.sqrt(second_maps[:, :, 0] ** 2 + second_maps[:, :, 1] ** 2 + MOD_EPSILON)
    local_cov = jnp.sum(cycle_weight * pair_mod * second_mod, axis=(2, 3)) / (ntheta * nphi)
    cov = lax.psum(local_cov, ("lat", "ord"))
    residual = (cov - target)[:, :, None, None]
    grad_second = (residual * cycle_weight * pair_mod / second_mod)[:, :, None] * second_maps
    grad_pair = (residual * cycle_weight * second_mod / pair_mod)[:, :, None] * pair_maps
    stacked = jnp.concatenate(
        [
            grad_second.reshape(2 * combos, phi_dev, cycle_dev),
            grad_pair.reshape(2 * combos, phi_dev, cycle_dev),
        ],
        axis=0,
    )
    back_first = reduce_degrees(grid_to_cycles(stacked), False, mix_backward_first)
    grad_mod = to_grid(back_first[:, :combos], expand_plain, True)
    grad_mod = grad_mod.reshape(pair_count, dir_count, phi_dev, cycle_dev)
    grad_first = (grad_mod / first_mod)[:, :, None] * first_maps
    back_second = reduce_degrees(
        grid_to_cycles(grad_first.reshape(2 * combos, phi_dev, cycle_dev)),
        False,
        mix_backward_second,
    )
    total = back_first[:, combos:] + back_second
    return to_grid(total, expand_plain, True)[0]


def solution(mesh):
    return jax.shard_map(
        shards,
        mesh=mesh,
        in_specs=(P("ord", "lat"), P("lat", "ord", None), P("lat"), P(), P(), P(), P(), P()),
        out_specs=P("ord", "lat"),
        check_vma=False,
    )
```

profile of v0, /device:TPU:0, one launch (start us, length us, event | category | flops | bytes accessed | tf_op | source)
XLA Modules:
  0.0 1201.6 jit_solution(1982683278580395780)
XLA Ops:
  8.1 7.1 all-to-all-start
  15.2 21.8 %fusion.47 = (f32[1,720,1440]{2,1,0:T(8,128)}, f32[1,720,1440]{2,1,0:T(8,128)}) fusion(s32[720]{0:T(1024)} %param.11), kind=kLoop, calls=%fused_computation.53 | loop fusion | flops 9331200 | bytes 8297280 | tf_op jit(solution)/shard_map/cos | solution.py:31
  38.4 10.2 fusion.119
  50.3 7.2 all-to-all-start.1
  57.7 7.4 all-to-all-done.1
  67.7 10.5 fusion.118
  80.0 55.5 %all-reduce.9.cloned.1.call-done = f32[720,1,2,45]{0,2,3,1:T(2,128)} async-done(((f32[720,1,2,45]{0,2,3,1:T(2,128)}), f32[720,1,2,45]{0,2,3,1:T(2,128)}) %all-reduce.9.cloned.1.call-update) | async-done | bytes 259216
  136.7 13.5 %all_gather.12 = f32[720,1,2,45]{3,2,1,0:T(2,128)S(1)} all-gather(f32[90,1,2,45]{3,2,1,0:T(2,128)S(1)} %copy.604), channel_id=1, replica_groups=mesh['lat'=8,'ord'=16] {'lat'}, dimensions={0}, use_global_device_ids=true | all-gather | bytes 291600 | tf_op jit(solution)/shard_map/all_gather | solution.py:69
  156.8 11.5 reshape.205
  168.3 19.1 %fusion.87 = f32[32,2,45,96]{3,0,1,2:T(8,128)} fusion(f32[720,32,2,45]{0,1,2,3:T(8,128)} %reshape.205, bf16[96,45,720]{2,0,1:T(8,128)(2,1)} %param.9, pred[45,720]{1,0:T(8,128)(4,1)S(1)} %iota_compare_fusion.1), kind=kOutput, calls=%fused_computation.72 | convolution fusion | flops 2395008000 | bytes 15653520 | tf_op jit(solution)/shard_map/rsl,lbqs->bqsr/dot_general | solution.py:71
  195.9 25.3 %all_to_all.270 = f32[16,1,17280]{2,1,0:T(1,128)S(1)} all-to-all(f32[16,1,17280]{2,1,0:T(1,128)} %reshape.263), channel_id=1, replica_groups=mesh['lat'=8,'ord'=16] {'ord'}, dimensions={0} | all-to-all | bytes 2211840 | tf_op jit(solution)/shard_map/all_to_all | solution.py:55
  237.5 9.3 fusion.58
  255.9 20.4 %all_to_all.271 = f32[16,1,17280]{2,1,0:T(1,128)S(1)} all-to-all(f32[16,1,17280]{2,1,0:T(1,128)S(1)} %reshape.265), channel_id=1, replica_groups=mesh['lat'=8,'ord'=16] {'ord'}, dimensions={0} | all-to-all | bytes 2211840 | tf_op jit(solution)/shard_map/all_to_all | solution.py:51
  290.9 12.5 %all_to_all.272 = f32[8,90,96]{1,0,2:T(8,128)S(1)} all-to-all(f32[8,90,96]{1,0,2:T(8,128)S(1)} %copy.623), channel_id=1, replica_groups=mesh['lat'=8,'ord'=16] {'ord'}, dimensions={2} | all-to-all | bytes 552960 | tf_op jit(solution)/shard_map/all_to_all | solution.py:46
  303.7 10.2 fusion.115
  317.8 7.2 reshape.267
  325.0 12.1 %all_to_all.273 = f32[16,1,4320]{2,1,0:T(1,128)S(1)} all-to-all(f32[16,1,4320]{2,1,0:T(1,128)S(1)} %reshape.267), channel_id=1, replica_groups=mesh['lat'=8,'ord'=16] {'ord'}, dimensions={0} | all-to-all | bytes 552960 | tf_op jit(solution)/shard_map/all_to_all | solution.py:42
  348.5 10.8 fusion.84
  359.6 62.8 %all-reduce.11.cloned.1.call-done = f32[720,8,2,45]{0,1,2,3:T(8,128)} async-done(((f32[720,8,2,45]{0,1,2,3:T(8,128)}), f32[720,8,2,45]{0,1,2,3:T(8,128)}) %all-reduce.11.cloned.1.call-update) | async-done | bytes 2073616
  425.7 38.2 %all-gather.4.cloned.1.call-done = f32[720,8,2,45]{3,1,2,0:T(8,128)} async-done(((f32[90,8,2,45]{3,1,2,0:T(8,128)}), f32[720,8,2,45]{3,1,2,0:T(8,128)}) %all-gather.4.cloned.1.call-update) | async-done | bytes 2073616 | tf_op jit(solution)/shard_map/all_gather | solution.py:69
  463.9 6.6 copy.629
  482.8 14.8 %fusion.96 = f32[16,2,45,96]{3,0,1,2:T(8,128)S(1)} fusion(f32[720,16,2,45]{0,1,2,3:T(8,128)} %reshape.208, bf16[96,45,720]{2,0,1:T(8,128)(2,1)} %param.9, pred[45,720]{1,0:T(8,128)(4,1)S(1)} %iota_compare_fusion.1), kind=kOutput, calls=%fused_computation.75 | convolution fusion | flops 1200614400 | bytes 10953360 | tf_op jit(solution)/shard_map/rsl,lbqs->bqsr/dot_general | solution.py:71
  501.3 19.4 %all_to_all.274 = f32[16,1,8640]{2,1,0:T(1,128)S(1)} all-to-all(f32[16,1,8640]{2,1,0:T(1,128)S(1)} %reshape.269), channel_id=1, replica_groups=mesh['lat'=8,'ord'=16] {'ord'}, dimensions={0} | all-to-all | bytes 1105920 | tf_op jit(solution)/shard_map/all_to_all | solution.py:55
  526.3 8.2 fusion.67
  549.3 9.4 all-to-all-done.7
  572.5 62.7 %psum.7 = f32[2,4]{1,0:T(2,128)S(1)} all-reduce(f32[2,4]{1,0:T(2,128)S(1)} %broadcast_multiply_fusion.2), channel_id=1, replica_groups=mesh['lat'=8,'ord'=16] {'lat','ord'}, use_global_device_ids=true, to_apply=%region_3.4 | all-reduce | flops 8 | bytes 64 | tf_op jit(solution)/shard_map/psum | solution.py:135
  642.8 26.1 %all_to_all.275 = f32[32,90,96]{1,0,2:T(8,128)S(1)} all-to-all(f32[32,90,96]{1,0,2:T(8,128)S(1)} %pad_maximum_fusion.1), channel_id=1, replica_groups=mesh['lat'=8,'ord'=16] {'ord'}, dimensions={2} | all-to-all | bytes 2211840 | tf_op jit(solution)/shard_map/all_to_all | solution.py:46
  670.5 11.9 fusion.93
  692.4 20.8 %all_to_all.276 = f32[16,1,17280]{2,1,0:T(1,128)S(1)} all-to-all(f32[16,1,17280]{2,1,0:T(1,128)S(1)} %reshape.273), channel_id=1, replica_groups=mesh['lat'=8,'ord'=16] {'ord'}, dimensions={0} | all-to-all | bytes 2211840 | tf_op jit(solution)/shard_map/all_to_all | solution.py:42
  730.2 14.7 %fusion.49 = f32[720,32,2,45]{0,1,2,3:T(8,128)} fusion(f32[32,2,45,96]{3,0,1,2:T(8,128)} %copy.647, bf16[96,45,720]{2,0,1:T(8,128)(2,1)} %param.9, pred[45,720]{1,0:T(8,128)(4,1)S(1)} %iota_compare_fusion.1), kind=kOutput, calls=%fused_computation.55 | convolution fusion | flops 2395008000 | bytes 15653520 | tf_op jit(solution)/shard_map/rsl,bqsr->lbqs/dot_general | solution.py:60
  745.6 103.4 %all-reduce.13.cloned.1.call-done = f32[720,32,2,45]{0,1,2,3:T(8,128)} async-done(((f32[720,32,2,45]{0,1,2,3:T(8,128)}), f32[720,32,2,45]{0,1,2,3:T(8,128)}) %all-reduce.13.cloned.1.call-update) | async-done | bytes 8294416
  855.1 39.1 %all-gather.6.cloned.1.call-done = f32[720,8,2,45]{3,1,2,0:T(8,128)} async-done(((f32[90,8,2,45]{3,1,2,0:T(8,128)}), f32[720,8,2,45]{3,1,2,0:T(8,128)}) %all-gather.6.cloned.1.call-update) | async-done | bytes 2073616 | tf_op jit(solution)/shard_map/all_gather | solution.py:69
  899.9 13.5 %fusion.108 = f32[8,2,45,96]{3,0,1,2:T(8,128)S(1)} fusion(f32[720,8,2,45]{0,1,2,3:T(8,128)S(1)} %copy.649, bf16[96,45,720]{2,0,1:T(8,128)(2,1)} %param.9, pred[45,720]{1,0:T(8,128)(4,1)S(1)} %iota_compare_fusion.1, f32[96]{0:T(128)S(1)} %copy-done.10), kind=kOutput, calls=%fused_computation.79 | convolution fusion | flops 603486720 | bytes 8603664 | tf_op jit(solution)/shard_map/rsl,lbqs->bqsr/dot_general | solution.py:71
  914.8 15.7 %all_to_all.277 = f32[16,1,4320]{2,1,0:T(1,128)S(1)} all-to-all(f32[16,1,4320]{2,1,0:T(1,128)S(1)} %reshape.275), channel_id=1, replica_groups=mesh['lat'=8,'ord'=16] {'ord'}, dimensions={0} | all-to-all | bytes 552960 | tf_op jit(solution)/shard_map/all_to_all | solution.py:55
  933.5 8.1 fusion.76
  949.8 12.0 %all_to_all.278 = f32[16,1,4320]{2,1,0:T(1,128)S(1)} all-to-all(f32[16,1,4320]{2,1,0:T(1,128)S(1)} %reshape.277), channel_id=1, replica_groups=mesh['lat'=8,'ord'=16] {'ord'}, dimensions={0} | all-to-all | bytes 552960 | tf_op jit(solution)/shard_map/all_to_all | solution.py:51
  971.4 15.9 %all_to_all.279 = f32[16,90,96]{1,0,2:T(8,128)S(1)} all-to-all(f32[16,90,96]{1,0,2:T(8,128)S(1)} %bitcast_multiply_fusion), channel_id=1, replica_groups=mesh['lat'=8,'ord'=16] {'ord'}, dimensions={2} | all-to-all | bytes 1105920 | tf_op jit(solution)/shard_map/all_to_all | solution.py:46
  988.1 10.6 fusion.102
  1002.6 6.6 reshape.279
  1009.2 14.3 %all_to_all.280 = f32[16,1,8640]{2,1,0:T(1,128)S(1)} all-to-all(f32[16,1,8640]{2,1,0:T(1,128)S(1)} %reshape.279), channel_id=1, replica_groups=mesh['lat'=8,'ord'=16] {'ord'}, dimensions={0} | all-to-all | bytes 1105920 | tf_op jit(solution)/shard_map/all_to_all | solution.py:42
  1037.0 11.7 fusion.81
  1051.7 67.5 %all-reduce.15.cloned.1.call-done = f32[720,16,2,45]{0,1,2,3:T(8,128)} async-done(((f32[720,16,2,45]{0,1,2,3:T(8,128)}), f32[720,16,2,45]{0,1,2,3:T(8,128)}) %all-reduce.15.cloned.1.call-update) | async-done | bytes 4147216
  1122.8 13.5 %all-gather = f32[720,2,45]{2,1,0:T(2,128)S(1)} all-gather(f32[90,2,45]{2,1,0:T(2,128)S(1)} %add.85), channel_id=2, replica_groups=mesh['lat'=8,'ord'=16] {'lat'}, dimensions={0}, use_global_device_ids=true | all-gather | bytes 291600 | tf_op jit(solution)/shard_map/all_gather | solution.py:69
  1137.1 13.5 %fusion.122 = f32[1,2,45,96]{3,1,2,0:T(2,128)S(1)} fusion(f32[720,2,45]{0,1,2:T(2,128)S(1)} %copy.663, bf16[96,45,720]{2,0,1:T(8,128)(2,1)} %param.9, pred[45,720]{1,0:T(8,128)(4,1)S(1)} %iota_compare_fusion.1, f32[96]{0:T(128)S(1)} %copy-done.10), kind=kOutput, calls=%fused_computation.88 | convolution fusion | flops 80879040 | bytes 6547344 | tf_op jit(solution)/shard_map/rsl,lbqs->bqsr/dot_general | solution.py:71
  1150.8 14.2 %all_to_all.281 = f32[16,1,540]{2,1,0:T(1,128)S(1)} all-to-all(f32[16,1,540]{2,1,0:T(1,128)S(1)} %reshape.281), channel_id=1, replica_groups=mesh['lat'=8,'ord'=16] {'ord'}, dimensions={0} | all-to-all | bytes 69120 | tf_op jit(solution)/shard_map/all_to_all | solution.py:55
  1166.1 6.9 fusion.80
  1173.9 6.8 reduce.22
  1181.1 10.8 all_to_all.282
  (197 shorter events, 235.0 us)
Async XLA Ops:
  6.5 31.5 %copy-start = (f32[8,720]{1,0:T(8,128)S(1)}, f32[8,720]{1,0:T(8,128)}, u32[]{:S(2)}) copy-start(f32[8,720]{1,0:T(8,128)} %param.12) | copy-start | bytes 69124
  8.1 30.2 %all-to-all-start = ((f32[1,90,96]{1,0,2:T(1,128)}), f32[1,90,96]{1,0,2:T(1,128)S(1)}, u32[]{:S(2)}, u32[]{:S(2)}) async-start(f32[1,90,96]{1,0,2:T(1,128)} %bitcast.4), calls=%async_computation | async-start | bytes 98304 | tf_op jit(solution)/shard_map/all_to_all | solution.py:46
  15.2 22.7 %copy-start.11 = (s32[2,2]{1,0:T(2,128)S(1)}, s32[2,2]{1,0:T(2,128)}, u32[]{:S(2)}) copy-start(s32[2,2]{1,0:T(2,128)} %param.14) | copy-start | bytes 52
  38.3 29.0 %copy-start.10 = (f32[96]{0:T(128)S(1)}, f32[96]{0:T(128)}, u32[]{:S(2)}) copy-start(f32[96]{0:T(128)} %param.10) | copy-start | bytes 1156
  50.3 14.9 %all-to-all-start.1 = ((f32[16,1,540]{2,1,0:T(1,128)}), f32[16,1,540]{2,1,0:T(1,128)S(1)}, u32[]{:S(2)}, u32[]{:S(2)}) async-start(f32[16,1,540]{2,1,0:T(1,128)} %reshape.261), calls=%async_computation.1 | async-start | bytes 81920 | tf_op jit(solution)/shard_map/all_to_all | solution.py:42
  57.5 78.0 %all-reduce.9.cloned.1.call-start = ((), (), s32[]{:S(2)}) async-start(), calls=%async_computation.18 | async-start | bytes 552960
  67.6 10.6 copy-start.13
  67.6 11.0 copy-start.14
  78.2 344.1 %all-reduce.11.cloned.1.call-start = ((), (), s32[]{:S(2)}) async-start(), calls=%async_computation.19 | async-start | bytes 4423680
  288.0 0.9 copy-start.2
  289.9 24.0 %copy-start.4 = (f32[2,4,1,90,96]{4,1,3,0,2:T(4,128)}, f32[2,4,1,90,96]{4,1,3,0,2:T(4,128)S(1)}, u32[]{:S(2)}) copy-start(f32[2,4,1,90,96]{4,1,3,0,2:T(4,128)S(1)} %copy.726) | copy-start | bytes 829444
  290.3 23.6 %copy-start.6 = (f32[2,4,1,90,96]{4,1,3,0,2:T(4,128)}, f32[2,4,1,90,96]{4,1,3,0,2:T(4,128)S(1)}, u32[]{:S(2)}) copy-start(f32[2,4,1,90,96]{4,1,3,0,2:T(4,128)S(1)} %copy.727) | copy-start | bytes 829444
  359.3 104.6 %all-gather.4.cloned.1.call-start = ((), (), s32[]{:S(2)}) async-start(), calls=%async_computation.16 | async-start | bytes 6635520 | tf_op jit(solution)/shard_map/all_gather | solution.py:69
  538.4 9.2 copy-start.8
  543.8 14.9 %all-to-all-start.7 = ((f32[16,1,8640]{2,1,0:T(1,128)}), f32[16,1,8640]{2,1,0:T(1,128)S(1)}, u32[]{:S(2)}, u32[]{:S(2)}) async-start(f32[16,1,8640]{2,1,0:T(1,128)} %reshape.271), calls=%async_computation.7 | async-start | bytes 1114112 | tf_op jit(solution)/shard_map/all_to_all | solution.py:51
  547.4 301.7 %all-reduce.13.cloned.1.call-start = ((), (), s32[]{:S(2)}) async-start(), calls=%async_computation.20 | async-start | bytes 17694720
  564.4 70.9 %copy-start.12 = (f32[2,4]{1,0:T(2,128)S(1)}, f32[2,4]{1,0:T(2,128)}, u32[]{:S(2)}) copy-start(f32[2,4]{1,0:T(2,128)} %param.15) | copy-start | bytes 100
  744.8 149.3 %all-gather.6.cloned.1.call-start = ((), (), s32[]{:S(2)}) async-start(), calls=%async_computation.17 | async-start | bytes 6635520 | tf_op jit(solution)/shard_map/all_gather | solution.py:69
  854.9 264.3 %all-reduce.15.cloned.1.call-start = ((), (), s32[]{:S(2)}) async-start(), calls=%async_computation.21 | async-start | bytes 8847360
  966.7 3.8 copy-start.5
  966.7 3.8 copy-start.7
  966.7 4.5 copy-start.3
  1048.6 1.1 copy-start.9
  1166.1 28.4 %copy-start.1 = (f32[8,720]{1,0:T(8,128)S(1)}, f32[8,720]{1,0:T(8,128)}, u32[]{:S(2)}) copy-start(f32[8,720]{1,0:T(8,128)} %param.12) | copy-start | bytes 69124
Sparse Core Ops, SparseCore 0:
  78.3 57.1 all-reduce.8
  359.4 62.8 all-reduce.10
  425.0 38.8 all-gather.3
  745.0 104.0 all-reduce.12
  855.0 39.1 all-gather.5
  1048.8 70.3 all-reduce.14
where the time goes:
time: 1210 us; the launch traced here: 1200 us
  waiting for transfers between devices  383 us (32%)
  blocking collectives  309 us (26%)
  local copies, waits for them, and re-layouts  216 us (18%)
  matrix products  188 us (16%)
  other arithmetic  70.8 us (6%)
  starting transfers between devices  18.7 us (2%)
  between operations  15.2 us (1%)
    unnamed x10, waiting for transfers between devices  289 us
    unnamed x68, local copies, waits for them, and re-layouts  90.7 us
    all_gather x2, waiting for transfers between devices, to_grid(): segment = lax.all_gather(coeffs, 'lat', axis=0, tiled=True)  77.2 us
    all_to_all x4, blocking collectives, cycles_to_grid(): lax.all_to_all(cycles, 'ord', split_axis=3, concat_axis=2, tiled=True)  74.7 us
    psum x1, blocking collectives, shards(): cov = lax.psum(local_cov, ('lat', 'ord'))  62.7 us
    dot_general x4, matrix products, to_grid(): jnp.einsum('rsl,lbqs->bqsr', legendre_rows, expanded, precision=HIGHEST_P...  60.9 us
    all_to_all x3, blocking collectives, grid_to_cycles(): lax.all_to_all(fields, 'ord', split_axis=2, concat_axis=1, tiled=True)  54.5 us
    dot_general x4, matrix products, harmonic_partials(): jnp.einsum('rsl,bqsr->lbqs', legendre_rows, source, precision=HIGHEST_PREC)  47.7 us
  transfers between devices with their start and end apart: 9, of which 8 were waited for; matrix products, arithmetic and copies ran while one was open for 2% of the time, Pallas kernels for 0%

commit v1 on v0

v1 whole, which is shorter than its diff:
```python
import functools
import math

import jax
import jax.numpy as jnp
from jax import lax
from jax.experimental import pallas as pl
from jax.experimental.pallas import tpu as pltpu
from jax.sharding import PartitionSpec as P

F32 = jnp.float32
BF16 = jnp.bfloat16
HIGHEST_PREC = lax.Precision.HIGHEST
MOD_EPSILON = 0.01
L = 720
NPHI = 1440
NTHETA = 768
LAT = 8
ORD = 16
SLOT = 45
SP = 48
SA = ORD * SP
LP = 768
KP = 768
SB = 8
STEPS = SP // SB
COV_ROW = SLOT
COV_STEP, COV_SUB = COV_ROW // SB, COV_ROW % SB
KT = 256
NORMING = math.sqrt(2.0 / NPHI)
VMEM = 50 * 1024 * 1024


def params(**kw):
    return pltpu.CompilerParams(vmem_limit_bytes=VMEM, **kw)


def lane_low(shape):
    return lax.broadcasted_iota(jnp.int32, shape, len(shape) - 1) % 128 < 64


def swap(x):
    return pltpu.roll(x, 64, x.ndim - 1)


def halves(first, second):
    low = lane_low(first.shape)
    return jnp.where(low, first, swap(second)), jnp.where(low, swap(first), second)


def split_rows(x):
    high = x.astype(BF16).astype(F32)
    return jnp.concatenate([high, x - high], axis=0).astype(BF16)


def dot(a, b):
    return lax.dot_general(a, b, (((1,), (0,)), ((), ())), preferred_element_type=F32)


def dot_t(a, b):
    return lax.dot_general(a, b, (((1,), (1,)), ((), ())), preferred_element_type=F32)


def analysis_one(x_ref, w_ref, m_ref, out_ref):
    w = w_ref[...]
    for s in range(SB):
        rows = x_ref[:, s, :] * w
        d = dot(split_rows(rows), m_ref[s])
        out_ref[:, s, :] = d[:2] + d[2:]


def analysis_fields(carry, x_ref, w_ref, m_ref, out_ref):
    w = w_ref[...]
    for s in range(SB):
        rows = x_ref[:, s, :]
        q0, q1 = halves(rows[:8], rows[8:])
        d = dot(split_rows(jnp.concatenate([q0 * w, q1 * w], axis=0)), m_ref[s])
        out_ref[0, s] = d[0:8] + d[16:24]
        out_ref[1, s] = d[8:16] + d[24:32]
    if carry:

        @pl.when(pl.program_id(0) == COV_STEP)
        def _():
            rows = x_ref[:, COV_SUB, :]
            total = (rows[:8] + rows[8:])[:, 0:1]
            out_ref[0, COV_SUB] = jnp.broadcast_to(total, (8, LP))


def analysis_sum(x_ref, kap_ref, m_ref, out_ref):
    kap = kap_ref[...]
    for s in range(SB):
        parts = []
        for w in range(2):
            rows = x_ref[:, w, s, :]
            parts += list(halves(rows[:8], rows[8:]))
        d = dot(split_rows(jnp.concatenate(parts, axis=0)), m_ref[s])
        d = d[:32] + d[32:]
        for q in range(2):
            both = d[8 * q : 8 * q + 8] * kap[0] + d[16 + 8 * q : 24 + 8 * q] * kap[1]
            out_ref[q, pl.ds(s, 1), :] = jnp.sum(both, axis=0, keepdims=True)


def in_order(core_ref, mine, other):
    even = core_ref[0] == 0
    return jnp.where(even, mine, other), jnp.where(even, other, mine)


def synthesis_first(core_ref, mine_ref, other_ref, kap_ref, m_ref, out_ref):
    kap = kap_ref[...]
    for s in range(SB):
        b0, b1 = in_order(core_ref, mine_ref[pl.ds(s, 1), :], other_ref[pl.ds(s, 1), :])
        rows = jnp.concatenate([kap[0] * b0, kap[0] * b1, kap[1] * b0, kap[1] * b1], axis=0)
        d = dot_t(split_rows(rows), m_ref[s])
        d = d[:32] + d[32:]
        for w in range(2):
            h0, h1 = halves(d[16 * w : 16 * w + 8], d[16 * w + 8 : 16 * w + 16])
            out_ref[:, w, s, :] = jnp.concatenate([h0, h1], axis=0)


def synthesis_fields(
    carry, core_ref, mine_ref, other_ref, kap_ref, w_ref, m_ref, mcov_ref, ocov_ref, target_ref, out_ref
):
    kap = kap_ref[...]
    w = w_ref[...]
    if carry:
        cov, _ = in_order(core_ref, mcov_ref[COV_SUB][:, 0:1], ocov_ref[COV_SUB][:, 0:1])
        residual = cov / (NTHETA * NPHI) - target_ref[...]
        kap = kap * residual
    for s in range(SB):
        b0, b1 = in_order(core_ref, mine_ref[s], other_ref[s])
        rows = jnp.concatenate([b0 * kap, b1 * kap], axis=0)
        d = dot_t(split_rows(rows), m_ref[s])
        d = (d[:16] + d[16:]) * w
        h0, h1 = halves(d[:8], d[8:])
        out_ref[:, s, :] = jnp.concatenate([h0, h1], axis=0)
    if carry:

        @pl.when(pl.program_id(0) == COV_STEP)
        def _():
            wide = jnp.broadcast_to(residual, (8, 128))
            out_ref[:, COV_SUB, :] = jnp.concatenate([wide, wide], axis=0)


def synthesis_last(core_ref, mine_ref, other_ref, w_ref, m_ref, out_ref):
    w = w_ref[...]
    for s in range(SB):
        b0, b1 = in_order(core_ref, mine_ref[pl.ds(s, 1), :], other_ref[pl.ds(s, 1), :])
        d = dot_t(split_rows(jnp.concatenate([b0, b1], axis=0)), m_ref[s])
        out_ref[:, s, :] = (d[:2] + d[2:]) * w


SMEM_SPEC = pl.BlockSpec(memory_space=pltpu.SMEM)


def whole(*shape):
    return pl.BlockSpec(shape, lambda i: (0,) * len(shape))


M_SPEC = pl.BlockSpec((SB, 128, LP), lambda i: (i, 0, 0))
ROW_SPEC = pl.BlockSpec((SB, LP), lambda i: (i, 0))


def cost(flops, nbytes):
    return pl.CostEstimate(flops=int(flops), bytes_accessed=int(nbytes), transcendentals=0)


def leg_cost(rows):
    return cost(2 * SP * rows * 128 * LP, SP * 128 * LP * 2 + SP * rows * LP * 2)


def run_analysis_one(x, w, m):
    return pl.pallas_call(
        analysis_one,
        grid=(STEPS,),
        in_specs=[pl.BlockSpec((2, SB, 128), lambda i: (0, i, 0)), whole(1, 128), M_SPEC],
        out_specs=pl.BlockSpec((2, SB, LP), lambda i: (0, i, 0)),
        out_shape=jax.ShapeDtypeStruct((2, SP, LP), F32),
        compiler_params=params(),
        cost_estimate=leg_cost(4),
        name="analysis_one",
    )(x, w, m)


def run_analysis_fields(x, w, m, carry):
    return pl.pallas_call(
        functools.partial(analysis_fields, carry),
        grid=(STEPS,),
        in_specs=[pl.BlockSpec((16, SB, 128), lambda i: (0, i, 0)), whole(1, 128), M_SPEC],
        out_specs=pl.BlockSpec((2, SB, 8, LP), lambda i: (0, i, 0, 0)),
        out_shape=jax.ShapeDtypeStruct((2, SP, 8, LP), F32),
        compiler_params=params(),
        cost_estimate=leg_cost(32),
        name="analysis_fields",
    )(x, w, m)


def run_analysis_sum(x, kap, m):
    return pl.pallas_call(
        analysis_sum,
        grid=(STEPS,),
        in_specs=[pl.BlockSpec((16, 2, SB, 128), lambda i: (0, 0, i, 0)), whole(2, 8, LP), M_SPEC],
        out_specs=pl.BlockSpec((2, SB, LP), lambda i: (0, i, 0)),
        out_shape=jax.ShapeDtypeStruct((2, SP, LP), F32),
        compiler_params=params(),
        cost_estimate=leg_cost(64),
        name="analysis_sum",
    )(x, kap, m)


def run_synthesis_first(core, mine, other, kap, m):
    return pl.pallas_call(
        synthesis_first,
        grid=(STEPS,),
        in_specs=[SMEM_SPEC, ROW_SPEC, ROW_SPEC, whole(2, 8, LP), M_SPEC],
        out_specs=pl.BlockSpec((16, 2, SB, 128), lambda i: (0, 0, i, 0)),
        out_shape=jax.ShapeDtypeStruct((16, 2, SP, 128), F32),
        compiler_params=params(),
        cost_estimate=leg_cost(64),
        name="synthesis_first",
    )(core, mine, other, kap, m)


def run_synthesis_fields(core, mine, other, kap, w, m, target, carry):
    field = pl.BlockSpec((SB, 8, LP), lambda i: (i, 0, 0))
    cov = pl.BlockSpec((SB, 8, 128), lambda i: (COV_STEP, 0, 0))
    return pl.pallas_call(
        functools.partial(synthesis_fields, carry),
        grid=(STEPS,),
        in_specs=[SMEM_SPEC, field, field, whole(8, LP), whole(1, 128), M_SPEC, cov, cov, whole(8, 1)],
        out_specs=pl.BlockSpec((16, SB, 128), lambda i: (0, i, 0)),
        out_shape=jax.ShapeDtypeStruct((16, SP, 128), F32),
        compiler_params=params(),
        cost_estimate=leg_cost(32),
        name="synthesis_fields",
    )(core, mine, other, kap, w, m, mine, other, target)


def run_synthesis_last(core, mine, other, w, m):
    return pl.pallas_call(
        synthesis_last,
        grid=(STEPS,),
        in_specs=[SMEM_SPEC, ROW_SPEC, ROW_SPEC, whole(1, 128), M_SPEC],
        out_specs=pl.BlockSpec((2, SB, 128), lambda i: (0, i, 0)),
        out_shape=jax.ShapeDtypeStruct((2, SP, 128), F32),
        compiler_params=params(),
        cost_estimate=leg_cost(4),
        name="synthesis_last",
    )(core, mine, other, w, m)


def store_split(x, high_ref, low_ref):
    high = x.astype(BF16)
    high_ref[...] = high
    low_ref[...] = (x - high.astype(F32)).astype(BF16)


def product(w_high, w_low, x_high, x_low):
    return dot(w_high, x_high) + dot(w_high, x_low) + dot(w_low, x_high)


def forward_step(values, high_w, low_w):
    high = values.astype(BF16)
    low = (values - high.astype(F32)).astype(BF16)
    return product(high_w, low_w, high, low)


def pack_parts(z, eta):
    low = lane_low(z.shape)
    other = swap(z)
    return jnp.where(low, z, other) * eta, jnp.where(low, other, z) * eta


def mod(maps):
    squares = maps * maps
    return jnp.sqrt(squares + swap(squares) + MOD_EPSILON)


def inverse_step(ic, iss, wch, wcl, wsh, wsl):
    even = product(wch[...], wcl[...], ic[0][...], ic[1][...])
    odd = product(wsh[...], wsl[...], iss[0][...], iss[1][...])
    return even + odd, even - odd


def accumulate(yc_ref, ys_ref, up, down, tch, tcl, tsh, tsl):
    c = forward_step(up + down, tch[...], tcl[...])
    s = forward_step(up - down, tsh[...], tsl[...])

    @pl.when(pl.program_id(0) == 0)
    def _():
        yc_ref[...] = c
        ys_ref[...] = s

    @pl.when(pl.program_id(0) > 0)
    def _():
        yc_ref[...] += c
        ys_ref[...] += s


def sum_parts(yc, ys, eta):
    vc, vs = yc * eta, ys * eta
    return jnp.where(lane_low(vc.shape), vc + swap(vc), vs + swap(vs))


def is_last():
    return pl.program_id(0) == pl.num_programs(0) - 1


def longitude_first(
    z_ref, eta_ref, wch, wcl, wsh, wsl, tch, tcl, tsh, tsl,
    out_ref, first_ref, pair_ref, ch, cl, sh, sl, yc, ys,
):
    @pl.when(pl.program_id(0) == 0)
    def _():
        eta = eta_ref[...]
        cs, ss = [], []
        for w in range(2):
            c, s = pack_parts(z_ref[:, w].reshape(SA, 128), eta)
            cs.append(c)
            ss.append(s)
        store_split(jnp.concatenate(cs, axis=1), ch, cl)
        store_split(jnp.concatenate(ss, axis=1), sh, sl)

    up, down = inverse_step((ch, cl), (sh, sl), wch, wcl, wsh, wsl)
    first_ref[0] = up[:, :128]
    first_ref[1] = down[:, :128]
    pair_ref[0] = up[:, 128:]
    pair_ref[1] = down[:, 128:]
    accumulate(yc, ys, mod(up[:, :128]), mod(down[:, :128]), tch, tcl, tsh, tsl)

    @pl.when(is_last())
    def _():
        out_ref[...] = jnp.where(lane_low((SA, 128)), yc[...], ys[...]).reshape(ORD, SP, 128)


def longitude_second(
    z_ref, eta_ref, weight_ref, fold_ref, pair_ref, wch, wcl, wsh, wsl, tch, tcl, tsh, tsl,
    out_ref, ratio_ref, ch, cl, sh, sl, yc, ys, cov,
):
    @pl.when(pl.program_id(0) == 0)
    def _():
        c, s = pack_parts(z_ref[...].reshape(SA, 128), eta_ref[...])
        store_split(c, ch, cl)
        store_split(s, sh, sl)
        cov[...] = jnp.zeros_like(cov)

    maps = inverse_step((ch, cl), (sh, sl), wch, wcl, wsh, wsl)
    weight = weight_ref[...]
    grads = []
    total = 0.0
    for i in range(2):
        second_mod = mod(maps[i])
        pair_mod = mod(pair_ref[i])
        total += pair_mod * second_mod
        grads.append(maps[i] * (weight * pair_mod / second_mod))
        ratio_ref[i] = pair_ref[i] * (weight * second_mod / pair_mod)
    cov[...] += jnp.sum(total * fold_ref[...], axis=0, keepdims=True) * weight
    accumulate(yc, ys, grads[0], grads[1], tch, tcl, tsh, tsl)

    @pl.when(is_last())
    def _():
        out = sum_parts(yc[...], ys[...], eta_ref[...]).reshape(ORD, SP, 128)
        lanes = lax.broadcasted_iota(jnp.int32, (1, 128), 1)
        value = jnp.sum(jnp.where(lanes < 64, cov[...], 0.0), axis=1, keepdims=True)
        rows = lax.broadcasted_iota(jnp.int32, (1, SP, 128), 1)
        out_ref[...] = jnp.where(rows == COV_ROW, value.reshape(1, 1, 1), out)


def longitude_third(
    z_ref, eta_ref, first_ref, ratio_ref, wch, wcl, wsh, wsl, tch, tcl, tsh, tsl,
    out_ref, ch, cl, sh, sl, yc, ys,
):
    @pl.when(pl.program_id(0) == 0)
    def _():
        c, s = pack_parts(z_ref[...].reshape(SA, 128), 1.0)
        store_split(c, ch, cl)
        store_split(s, sh, sl)

    maps = inverse_step((ch, cl), (sh, sl), wch, wcl, wsh, wsl)
    residual = z_ref[0, pl.ds(COV_ROW, 1), 0:1]
    grads = []
    for i in range(2):
        first = first_ref[i]
        grads.append(
            jnp.concatenate([first * (maps[i] / mod(first)), ratio_ref[i] * residual], axis=1)
        )
    accumulate(yc, ys, grads[0], grads[1], tch, tcl, tsh, tsl)

    @pl.when(is_last())
    def _():
        eta = eta_ref[...]
        for w in range(2):
            part = slice(128 * w, 128 * w + 128)
            out_ref[:, w] = sum_parts(yc[:, part], ys[:, part], eta).reshape(ORD, SP, 128)


W_SPEC = pl.BlockSpec((KT, SA), lambda i: (i, 0))
T_SPEC = pl.BlockSpec((SA, KT), lambda i: (0, i))
MAP_SPEC = pl.BlockSpec((2, KT, 128), lambda i: (0, i, 0))
MAP_SHAPE = jax.ShapeDtypeStruct((2, KP, 128), F32)


def lon_scratch(n_in, n_out):
    return [pltpu.VMEM((SA, n_in), BF16)] * 4 + [pltpu.VMEM((SA, n_out), F32)] * 2


def lon_cost(n_in, n_out):
    return cost(12 * KP * SA * (n_in + n_out), 8 * KP * SA * 2 + 3 * KP * 128 * 4)


def run_longitude_first(z, eta, waves):
    return pl.pallas_call(
        longitude_first,
        grid=(KP // KT,),
        in_specs=[whole(ORD, 2, SP, 128), whole(SA, 128)] + [W_SPEC] * 4 + [T_SPEC] * 4,
        out_specs=[whole(ORD, SP, 128), MAP_SPEC, MAP_SPEC],
        out_shape=[jax.ShapeDtypeStruct((ORD, SP, 128), F32), MAP_SHAPE, MAP_SHAPE],
        scratch_shapes=lon_scratch(256, 128),
        compiler_params=params(),
        cost_estimate=lon_cost(256, 128),
        name="longitude_first",
    )(z, eta, *waves)


def run_longitude_second(z, eta, weight, fold, pair, waves):
    return pl.pallas_call(
        longitude_second,
        grid=(KP // KT,),
        in_specs=[
            whole(ORD, SP, 128), whole(SA, 128), whole(1, 128),
            pl.BlockSpec((KT, 128), lambda i: (i, 0)), MAP_SPEC,
        ]
        + [W_SPEC] * 4
        + [T_SPEC] * 4,
        out_specs=[whole(ORD, SP, 128), MAP_SPEC],
        out_shape=[jax.ShapeDtypeStruct((ORD, SP, 128), F32), MAP_SHAPE],
        scratch_shapes=lon_scratch(128, 128) + [pltpu.VMEM((1, 128), F32)],
        compiler_params=params(),
        cost_estimate=lon_cost(128, 128),
        name="longitude_second",
    )(z, eta, weight, fold, pair, *waves)


def run_longitude_third(z, eta, first, ratio, waves):
    return pl.pallas_call(
        longitude_third,
        grid=(KP // KT,),
        in_specs=[whole(ORD, SP, 128), whole(SA, 128), MAP_SPEC, MAP_SPEC]
        + [W_SPEC] * 4
        + [T_SPEC] * 4,
        out_specs=whole(ORD, 2, SP, 128),
        out_shape=jax.ShapeDtypeStruct((ORD, 2, SP, 128), F32),
        scratch_shapes=lon_scratch(128, 256),
        compiler_params=params(),
        cost_estimate=lon_cost(128, 256),
        name="longitude_third",
    )(z, eta, first, ratio, *waves)


def split_array(x):
    high = lax.reduce_precision(x, 8, 7)
    return high.astype(BF16), (x - high).astype(BF16)


def angle(product_of):
    return (product_of % NPHI).astype(F32) * (2.0 * math.pi / NPHI)


def make_waves(slots, valid):
    scale = jnp.where(valid, NORMING, 0.0).astype(F32)
    coarse = jnp.arange(KP // 32, dtype=jnp.int32)[:, None] * 32 * slots[None, :]
    fine = jnp.arange(32, dtype=jnp.int32)[:, None] * slots[None, :]
    ca, sa = jnp.cos(angle(coarse)) * scale, jnp.sin(angle(coarse)) * scale
    cb, sb = jnp.cos(angle(fine)), jnp.sin(angle(fine))
    ca, sa, cb, sb = lax.optimization_barrier((ca, sa, cb, sb))
    keep = (jnp.arange(KP) <= NPHI // 2)[:, None]
    wc = jnp.where(keep, (ca[:, None] * cb[None] - sa[:, None] * sb[None]).reshape(KP, SA), 0.0)
    ws = jnp.where(keep, (sa[:, None] * cb[None] + ca[:, None] * sb[None]).reshape(KP, SA), 0.0)
    coarse = jnp.arange(KP // 128, dtype=jnp.int32)[None, :] * 128 * slots[:, None]
    fine = jnp.arange(128, dtype=jnp.int32)[None, :] * slots[:, None]
    ca, sa = jnp.cos(angle(coarse)) * scale[:, None], jnp.sin(angle(coarse)) * scale[:, None]
    cb, sb = jnp.cos(angle(fine)), jnp.sin(angle(fine))
    ca, sa, cb, sb = lax.optimization_barrier((ca, sa, cb, sb))
    fold = fold_weights()[None, :]
    tc = jnp.concatenate([ca[:, i : i + 1] * cb - sa[:, i : i + 1] * sb for i in range(KP // 128)], axis=1)
    ts = jnp.concatenate([sa[:, i : i + 1] * cb + ca[:, i : i + 1] * sb for i in range(KP // 128)], axis=1)
    arrays = []
    for table in (wc, ws, tc * fold, ts * fold):
        arrays += list(split_array(table))
    return lax.optimization_barrier(tuple(arrays))


def fold_weights():
    k = jnp.arange(KP)
    half = NPHI // 2
    return jnp.where((k == 0) | (k == half), 0.5, jnp.where(k < half, 1.0, 0.0)).astype(F32)


def pad_cycles(x):
    lead = x.shape[:-1]
    x = x.reshape(lead + (2, 48))
    return jnp.pad(x, [(0, 0)] * len(lead) + [(0, 0), (0, 16)]).reshape(lead + (128,))


def pad_degrees(x):
    return jnp.pad(x, [(0, 0)] * (x.ndim - 1) + [(0, LP - L)])


def ord_exchange(x):
    return lax.all_to_all(x, "ord", split_axis=0, concat_axis=0, tiled=True)


def ord_gather(x):
    return ord_exchange(jnp.broadcast_to(x[None], (ORD,) + x.shape))


Z_GROUPS = [[0, 2, 4, 6], [1, 3, 5, 7]]


def z_exchange(x):
    return lax.all_to_all(x, "lat", split_axis=0, concat_axis=0, tiled=True, axis_index_groups=Z_GROUPS)


def core_swap(x):
    return lax.ppermute(x, "lat", [(i, i ^ 1) for i in range(LAT)])


def z_shift(x, step):
    return lax.ppermute(x, "lat", [(i, (i + 2 * step) % LAT) for i in range(LAT)])


def core_sum(parts, core):
    mine = lax.dynamic_index_in_dim(parts, core, 0, keepdims=False)
    away = lax.dynamic_index_in_dim(parts, 1 - core, 0, keepdims=False)
    return mine + core_swap(away)


def lat_sum_small(parts, core):
    mine = core_sum(parts, core)
    mine = mine + z_shift(mine, 1) + z_shift(mine, 3) + z_shift(mine, 2)
    return mine, core_swap(mine)


def lat_sum_large(parts, core):
    mine = core_sum(parts, core)
    blocks = z_exchange(mine.reshape(4, SP // 4, 8, LP))
    block = blocks[0] + blocks[1] + blocks[2] + blocks[3]
    mine = z_exchange(jnp.broadcast_to(block[None], (4,) + block.shape)).reshape(SP, 8, LP)
    return mine, core_swap(mine)


def shards(grid_field, legendre, cycle_weight, slot_order, kappa, eta, pairs, target):
    me = lax.axis_index("ord")
    core = lax.axis_index("lat") % 2
    core_flag = core.astype(jnp.int32).reshape(1)
    direction = me % 4

    field = jnp.pad(pad_cycles(grid_field), [(0, 6), (0, 0)])
    field_all = ord_gather(field).reshape(ORD * 96, 128)

    slots2 = jnp.pad(slot_order.reshape(ORD, SLOT), [(0, 0), (0, SP - SLOT)])
    valid2 = jnp.broadcast_to(jnp.arange(SP) < SLOT, (ORD, SP))
    slots, valid = slots2.reshape(SA), valid2.reshape(SA)
    my_slots = lax.dynamic_index_in_dim(slots2, me, 0, keepdims=False)
    own_valid = jnp.arange(SP) < SLOT
    degree_ids = jnp.arange(L, dtype=jnp.int32)
    table = jnp.where(degree_ids[None, None, :] >= my_slots[None, :SLOT, None], legendre, jnp.zeros((), BF16))
    table = jnp.transpose(table, (1, 0, 2)).reshape(SLOT, 2, 48, L)
    table = jnp.pad(table, [(0, SP - SLOT), (0, 0), (0, 16), (0, LP - L)]).reshape(SP, 128, LP)

    offset = jnp.arange(96, dtype=jnp.int32)
    longitude = (jnp.arange(ORD, dtype=jnp.int32)[:, None] * 90 + offset[None, :]).reshape(ORD * 96)
    k_valid = jnp.broadcast_to(offset < 90, (ORD, 96)).reshape(ORD * 96)
    phase = angle(my_slots[:, None] * longitude[None, :])
    own_scale = jnp.where(own_valid[:, None] & k_valid[None, :], NORMING, 0.0).astype(F32)
    own_waves = jnp.stack([jnp.cos(phase) * own_scale, jnp.sin(phase) * own_scale]).reshape(2 * SP, ORD * 96)

    phase = angle((me * 90 + offset)[:, None] * slots[None, :])
    end_scale = jnp.where(valid[None, :], NORMING, 0.0).astype(F32)
    end_waves = jnp.stack(
        [(jnp.cos(phase) * end_scale).reshape(96, ORD, SP), (jnp.sin(phase) * end_scale).reshape(96, ORD, SP)], axis=2
    ).reshape(96, ORD * 2 * SP)

    waves = make_waves(slots, valid)
    eta_rows = lax.dynamic_index_in_dim(eta, direction, 0, keepdims=False)
    hit = slots[:, None] == degree_ids[None, :]
    eta_cols = [jnp.sum(jnp.where(hit, eta_rows[r][None, :], 0.0), axis=1, keepdims=True) for r in range(2)]
    eta_lanes = jnp.where(jnp.arange(128)[None, :] < 64, eta_cols[0], eta_cols[1])

    scale_ids = jnp.arange(kappa.shape[0], dtype=jnp.int32)
    picks = [(pairs[:, i : i + 1] == scale_ids[None, :]).astype(F32) for i in range(2)]
    kaps = [pad_degrees(jnp.sum(pick[:, :, None] * kappa[None], axis=1)) for pick in picks]
    kap_rows = jnp.stack([jnp.repeat(kap, 4, axis=0) for kap in kaps])
    kap_second = kap_rows[1]
    target_rows = target.reshape(8, 1)

    weight_lanes = pad_cycles(cycle_weight[None, :])
    ones = jnp.ones((1, 128), F32)
    weight_halves = weight_lanes.reshape(2, 64)
    my_weight = lax.dynamic_index_in_dim(weight_halves, me // 8, 0, keepdims=True)
    my_weight = jnp.concatenate([my_weight, my_weight], axis=1)
    fold_lanes = jnp.broadcast_to(fold_weights()[:, None], (KP, 128))

    spectra = jnp.dot(own_waves, field_all, precision=HIGHEST_PREC).reshape(2, SP, 128)
    mine, other = lat_sum_small(run_analysis_one(spectra, weight_lanes, table), core)
    z_first = ord_exchange(run_synthesis_first(core_flag, mine, other, kap_rows, table))
    spectra, first_maps, pair_maps = run_longitude_first(z_first, eta_lanes, waves)
    parts = run_analysis_fields(ord_exchange(spectra), weight_lanes, table, False)
    mine, other = lat_sum_large(parts, core)
    z_second = ord_exchange(
        run_synthesis_fields(core_flag, mine, other, kap_second, ones, table, target_rows, False)
    )
    spectra, ratio = run_longitude_second(z_second, eta_lanes, my_weight, fold_lanes, pair_maps, waves)
    parts = run_analysis_fields(ord_exchange(spectra), ones, table, True)
    mine, other = lat_sum_large(parts, core)
    z_third = ord_exchange(
        run_synthesis_fields(core_flag, mine, other, kap_second, weight_lanes, table, target_rows, True)
    )
    spectra = run_longitude_third(z_third, eta_lanes, first_maps, ratio, waves)
    mine, other = lat_sum_small(run_analysis_sum(ord_exchange(spectra), kap_rows, table), core)
    cycles = run_synthesis_last(core_flag, mine, other, weight_lanes, table)
    cycles_all = ord_gather(cycles.reshape(2 * SP, 128)).reshape(ORD * 2 * SP, 128)
    result = jnp.dot(end_waves, cycles_all, precision=HIGHEST_PREC)
    return result[:90].reshape(90, 2, 64)[:, :, :48].reshape(90, 96)


def solution(mesh):
    return jax.shard_map(
        shards,
        mesh=mesh,
        in_specs=(P("ord", "lat"), P("lat", "ord", None), P("lat"), P(), P(), P(), P(), P()),
        out_specs=P("ord", "lat"),
        check_vma=False,
    )
```

time: 1210 us -> 352 us (0.29)
  waiting for transfers between devices: 383 us -> 59.4 us
  local copies, waits for them, and re-layouts: 216 us -> 19.5 us
  matrix products: 188 us -> 2.17 us
  blocking collectives: 309 us -> 131 us
  Pallas kernels: 0 us -> 79.1 us
  other arithmetic: 70.8 us -> 26.2 us
  between operations: 15.2 us -> 0.75 us
  starting transfers between devices: 18.7 us -> 31.7 us
    unnamed x10 -> x0, waiting for transfers between devices: 289 us -> none
    dot_general x21 -> x1, matrix products: 188 us -> 0.72 us  [shards(): jnp.dot(own_waves, field_all, precision=HIGHEST_PREC).reshape(2, SP, 128)]
    all_to_all x13 -> x8, blocking collectives: 219 us -> 131 us  [the longest x4 76 us: z_exchange(): lax.all_to_all(x, 'lat', split_axis=0, concat_axis=0, tiled=True, axis_in...]
    unnamed x68 -> x37, local copies, waits for them, and re-layouts: 90.7 us -> 4.39 us
    pallas_call x0 -> x11, Pallas kernels: none -> 79.1 us  [the longest x2 15.4 us: run_synthesis_fields(): pl.pallas_call(functools.partial(synthesis_fields, carry), grid=(STEPS,),...]
    all_gather x2 -> x0, waiting for transfers between devices: 77.2 us -> none  [to_grid(): segment = lax.all_gather(coeffs, 'lat', axis=0, tiled=True)]
    psum x1 -> x0, blocking collectives: 62.7 us -> none  [shards(): cov = lax.psum(local_cov, ('lat', 'ord'))]
    all_to_all x26 -> x0, local copies, waits for them, and re-layouts: 44.4 us -> none  [the longest x8 20.9 us: longitude_forward(): lax.all_to_all(spectra, 'ord', split_axis=2, concat_axis=3, tiled=True)]
  transfers between devices with their start and end apart: 9 -> 18, of which waited for: 8 -> 15; matrix products, arithmetic and copies ran while one was open for 2% -> 11% of each run, Pallas kernels for 0% -> 0%
where the time goes in v1:
time: 352 us; the launch traced here: 350 us
  blocking collectives  131 us (37%)
  Pallas kernels  79.1 us (22%)
  waiting for transfers between devices  59.4 us (17%)
  starting transfers between devices  31.7 us (9%)
  other arithmetic  26.2 us (7%)
  local copies, waits for them, and re-layouts  19.5 us (6%)
    all_to_all x4, blocking collectives, z_exchange(): lax.all_to_all(x, 'lat', split_axis=0, concat_axis=0, tiled=True, axis_in...  76 us
    all_to_all x4, blocking collectives, ord_exchange(): return lax.all_to_all(x, 'ord', split_axis=0, concat_axis=0, tiled=True)  55.4 us
    all_to_all x4, waiting for transfers between devices, ord_exchange(): return lax.all_to_all(x, 'ord', split_axis=0, concat_axis=0, tiled=True)  30.8 us
    all_to_all x4, starting transfers between devices, ord_exchange(): return lax.all_to_all(x, 'ord', split_axis=0, concat_axis=0, tiled=True)  21.7 us
    pallas_call x2, Pallas kernels, run_synthesis_fields(): pl.pallas_call(functools.partial(synthesis_fields, carry), grid=(STEPS,),...  15.4 us
    ppermute x8, waiting for transfers between devices, core_swap(): return lax.ppermute(x, 'lat', [(i, i ^ 1) for i in range(LAT)])  15.2 us
    ppermute x6, waiting for transfers between devices, z_shift(): lax.ppermute(x, 'lat', [(i, (i + 2 * step) % LAT) for i in range(LAT)])  13.5 us
    pallas_call x2, Pallas kernels, run_analysis_fields(): pl.pallas_call(functools.partial(analysis_fields, carry), grid=(STEPS,),...  12.5 us
  transfers between devices with their start and end apart: 18, of which 15 were waited for; matrix products, arithmetic and copies ran while one was open for 11% of the time, Pallas kernels for 0%

profile of v1, /device:TPU:0, one launch (start us, length us, event | category | flops | bytes accessed | tf_op | source)
XLA Modules:
  0.0 350.2 jit_solution(10599349392888966352)
XLA Ops:
  2.1 7.1 %all-to-all-start = ((f32[16,96,128]{2,1,0:T(8,128)}), f32[16,96,128]{2,1,0:T(8,128)S(1)}, u32[]{:S(2)}, u32[]{:S(2)}) async-start(f32[16,96,128]{2,1,0:T(8,128)} %broadcast_in_dim.207), calls=%async_computation | async-start | bytes 1572864 | tf_op jit(solution)/shard_map/all_to_all | solution.py:509
  9.4 1.7 fusion.16
  13.8 6.2 %broadcast_select_fusion = bf16[96,45,720]{2,0,1:T(8,128)(2,1)} fusion(bf16[96,45,720]{2,0,1:T(8,128)(2,1)} %param.9, pred[45,720]{1,0:T(8,128)(4,1)S(1)} %iota_compare_fusion.1), kind=kLoop, calls=%fused_computation | loop fusion | flops 3110400 | bytes 12474000 | tf_op jit(solution)/shard_map/jit(_where)/select_n | solution.py:566
  20.0 8.0 %pad.31 = bf16[48,2,64,768]{3,2,1,0:T(8,128)(2,1)} pad(bf16[45,2,48,720]{3,2,1,0:T(8,128)(2,1)} %bitcast.74, bf16[]{:T(256)} %constant.159.clone.1), padding=0_3x0_0x0_16x0_48 | pad | bytes 15657986 | tf_op jit(solution)/shard_map/jit(_pad)/pad | solution.py:568
  29.6 2.7 fusion.3
  32.3 2.9 multiply_add_fusion
  37.3 6.0 %analysis_one.1 = f32[2,48,768]{2,1,0:T(8,128)S(1)} custom-call(f32[2,48,128]{2,1,0:T(8,128)S(1)} %fusion.6.x_ref, f32[1,128]{1,0:T(1,128)S(1)} %reshape.547.w_ref, bf16[48,128,768]{2,1,0:T(8,128)(2,1)} %bitcast.66), custom_call_target="tpu_custom_call" | custom-call | flops 37748736 | bytes 9732096 | tf_op jit(solution)/shard_map/analysis_one/pallas_call | solution.py:172
  44.7 2.0 collective-permute-start.1
  46.7 2.2 collective-permute-start.2
  48.9 1.8 collective-permute-start.3
  50.9 2.1 collective-permute-done.1
  53.0 2.5 collective-permute-done.2
  55.5 1.8 collective-permute-done.3
  59.0 8.2 %synthesis_first.1 = f32[16,2,48,128]{3,2,1,0:T(8,128)} custom-call(s32[1]{0:T(128)} %bitcast.1.core_ref, f32[48,768]{1,0:T(8,128)S(1)} %add_add_fusion.1.mine_ref, f32[48,768]{1,0:T(8,128)S(1)} %collective-permute-done.4.other_ref, f32[2,8,768]{2,1,0:T(8,128)S(1)} %constant_dynamic-update-slice_fusion.kap_ref, bf16[48,128,768]{2,1,0:T(8,128)(2,1)} %bitcast.67), custom_call_target="tpu_custom_call" | custom-call | flops 603979776 | bytes 14155776 | tf_op jit(solution)/shard_map/synthesis_first/pallas_call | solution.py:211
  67.2 7.2 %all-to-all-start.1 = ((f32[16,2,48,128]{3,2,1,0:T(8,128)}), f32[16,2,48,128]{3,2,1,0:T(8,128)S(1)}, u32[]{:S(2)}, u32[]{:S(2)}) async-start(f32[16,2,48,128]{3,2,1,0:T(8,128)} %synthesis_first.1), calls=%async_computation.1 | async-start | bytes 1572864 | tf_op jit(solution)/shard_map/all_to_all | solution.py:509
  74.4 5.2 %fusion.1 = (bf16[768,768]{1,0:T(8,128)(2,1)}, bf16[768,768]{1,0:T(8,128)(2,1)}, bf16[768,768]{1,0:T(8,128)(2,1)}, bf16[768,768]{1,0:T(8,128)(2,1)}) fusion(f32[24,32,768]{2,1,0:T(8,128)} %get-tuple-element.87, pred[768]{0:T(1024)(128)(4,1)S(1)} %iota_compare_fusion.5, f32[24,32,768]{2,1,0:T(8,128)} %get-tuple-element.88), kind=kLoop, calls=%fused_computation.10 | loop fusion | flops 5898240 | bytes 9437952 | tf_op jit(solution)/shard_map/convert_element_type | solution.py:461
  81.2 8.1 %all-to-all-done.1.z_ref = f32[16,2,48,128]{3,2,1,0:T(8,128)S(1)} async-done(((f32[16,2,48,128]{3,2,1,0:T(8,128)}), f32[16,2,48,128]{3,2,1,0:T(8,128)S(1)}, u32[]{:S(2)}, u32[]{:S(2)}) %all-to-all-start.1) | async-done | bytes 786464 | tf_op jit(solution)/shard_map/all_to_all | solution.py:509
  89.3 7.8 %longitude_first.1 = (f32[16,48,128]{2,1,0:T(8,128)S(1)}, f32[2,768,128]{2,1,0:T(8,128)S(1)}, f32[2,768,128]{2,1,0:T(8,128)S(1)}) custom-call(f32[16,2,48,128]{3,2,1,0:T(8,128)S(1)} %all-to-all-done.1.z_ref, f32[768,128]{1,0:T(8,128)S(1)} %broadcast_select_fusion.1.eta_ref, bf16[768,768]{1,0:T(8,128)(2,1)} %get-tuple-element.34.wch, ...), custom_call_target="tpu_custom_call" | custom-call | flops 2717908992 | bytes 10616832 | tf_op jit(solution)/shard_map/longitude_first/pallas_call | solution.py:411
  98.0 12.3 %all_to_all.60.x_ref = f32[16,48,128]{2,1,0:T(8,128)S(1)} all-to-all(f32[16,48,128]{2,1,0:T(8,128)S(1)} %get-tuple-element.42), channel_id=1, replica_groups=mesh['lat'=8,'ord'=16] {'ord'}, dimensions={0} | all-to-all | bytes 786432 | tf_op jit(solution)/shard_map/all_to_all | solution.py:509
  110.3 6.2 %analysis_fields.2 = f32[2,48,8,768]{3,2,1,0:T(8,128)S(1)} custom-call(f32[16,48,128]{2,1,0:T(8,128)S(1)} %all_to_all.60.x_ref, f32[1,128]{1,0:T(1,128)S(1)} %reshape.547.w_ref, bf16[48,128,768]{2,1,0:T(8,128)(2,1)} %bitcast.68), custom_call_target="tpu_custom_call" | custom-call | flops 301989888 | bytes 11796480 | tf_op jit(solution)/shard_map/analysis_fields/pallas_call | solution.py:185
  116.7 2.8 collective-permute-done.5
  119.7 19.7 %all_to_all.61 = f32[4,12,8,768]{3,2,1,0:T(8,128)S(1)} all-to-all(f32[4,12,8,768]{3,2,1,0:T(8,128)S(1)} %bitcast.75), channel_id=1, replica_groups={{0,32,64,96},{16,48,80,112},{1,33,65,97},{17,49,81,113},{2,34,66,98},{1..., dimensions={0} | all-to-all | bytes 2359296 | tf_op jit(solution)/shard_map/all_to_all | solution.py:520
  139.6 18.1 %all_to_all.62 = f32[4,12,8,768]{3,2,1,0:T(8,128)S(1)} all-to-all(f32[4,12,8,768]{3,2,1,0:T(8,128)S(1)} %broadcast_in_dim.227), channel_id=1, replica_groups={{0,32,64,96},{16,48,80,112},{1,33,65,97},{17,49,81,113},{2,34,66,98},{1..., dimensions={0} | all-to-all | bytes 2359296 | tf_op jit(solution)/shard_map/all_to_all | solution.py:520
  157.6 1.4 squeeze_stack_reshape.3.kap_ref
  159.1 1.4 collective-permute-done.6.other_ref.ocov_ref
  161.2 7.9 %synthesis_fields.2 = f32[16,48,128]{2,1,0:T(8,128)} custom-call(s32[1]{0:T(128)} %bitcast.1.core_ref, f32[48,8,768]{2,1,0:T(8,128)S(1)} %bitcast.60, f32[48,8,768]{2,1,0:T(8,128)S(1)} %collective-permute-done.6.other_ref.ocov_ref, f32[8,768]{1,0:T(8,128)S(1)} %copy-done.4, f32[1,128]{1,0:T(1,128)S(1)} %broadcast_in_dim.228.w_ref, ...), custom_call_target="tpu_custom_call" | custom-call | flops 301989888 | bytes 11796480 | tf_op jit(solution)/shard_map/synthesis_fields/pallas_call | solution.py:226
  169.2 3.7 %all-to-all-start.5 = ((f32[16,48,128]{2,1,0:T(8,128)}), f32[16,48,128]{2,1,0:T(8,128)S(1)}, u32[]{:S(2)}, u32[]{:S(2)}) async-start(f32[16,48,128]{2,1,0:T(8,128)} %synthesis_fields.2), calls=%async_computation.5 | async-start | bytes 786432 | tf_op jit(solution)/shard_map/all_to_all | solution.py:509
  173.7 9.4 %all-to-all-done.5.z_ref = f32[16,48,128]{2,1,0:T(8,128)S(1)} async-done(((f32[16,48,128]{2,1,0:T(8,128)}), f32[16,48,128]{2,1,0:T(8,128)S(1)}, u32[]{:S(2)}, u32[]{:S(2)}) %all-to-all-start.5) | async-done | bytes 393248 | tf_op jit(solution)/shard_map/all_to_all | solution.py:509
  184.4 8.2 %longitude_second.1 = (f32[16,48,128]{2,1,0:T(8,128)S(1)}, f32[2,768,128]{2,1,0:T(8,128)S(1)}) custom-call(f32[16,48,128]{2,1,0:T(8,128)S(1)} %all-to-all-done.5.z_ref, f32[768,128]{1,0:T(8,128)S(1)} %broadcast_select_fusion.1.eta_ref, f32[1,128]{1,0:T(1,128)S(1)} %pad_maximum_fusion.1.weight_ref, f32[768,128]{1,0:T(8,128)S(1)} %broadcast_in_dim.229.fold_ref, ...), custom_call_target="tpu_custom_call" | custom-call | flops 1811939328 | bytes 10616832 | tf_op jit(solution)/shard_map/longitude_second/pallas_call | solution.py:425
  192.6 12.7 %all_to_all.63.x_ref = f32[16,48,128]{2,1,0:T(8,128)S(1)} all-to-all(f32[16,48,128]{2,1,0:T(8,128)S(1)} %get-tuple-element.44), channel_id=1, replica_groups=mesh['lat'=8,'ord'=16] {'ord'}, dimensions={0} | all-to-all | bytes 786432 | tf_op jit(solution)/shard_map/all_to_all | solution.py:509
  205.3 6.3 %analysis_fields.3 = f32[2,48,8,768]{3,2,1,0:T(8,128)S(1)} custom-call(f32[16,48,128]{2,1,0:T(8,128)S(1)} %all_to_all.63.x_ref, f32[1,128]{1,0:T(1,128)S(1)} %broadcast_in_dim.228.w_ref, bf16[48,128,768]{2,1,0:T(8,128)(2,1)} %bitcast.70), custom_call_target="tpu_custom_call" | custom-call | flops 301989888 | bytes 11796480 | tf_op jit(solution)/shard_map/analysis_fields/pallas_call | solution.py:185
  211.8 2.8 collective-permute-done.7
  214.7 19.5 %all_to_all.64 = f32[4,12,8,768]{3,2,1,0:T(8,128)S(1)} all-to-all(f32[4,12,8,768]{3,2,1,0:T(8,128)S(1)} %bitcast.76), channel_id=1, replica_groups={{0,32,64,96},{16,48,80,112},{1,33,65,97},{17,49,81,113},{2,34,66,98},{1..., dimensions={0} | all-to-all | bytes 2359296 | tf_op jit(solution)/shard_map/all_to_all | solution.py:520
  234.4 18.7 %all_to_all.65 = f32[4,12,8,768]{3,2,1,0:T(8,128)S(1)} all-to-all(f32[4,12,8,768]{3,2,1,0:T(8,128)S(1)} %broadcast_in_dim.231), channel_id=1, replica_groups={{0,32,64,96},{16,48,80,112},{1,33,65,97},{17,49,81,113},{2,34,66,98},{1..., dimensions={0} | all-to-all | bytes 2359296 | tf_op jit(solution)/shard_map/all_to_all | solution.py:520
  253.1 2.8 collective-permute-done.8.other_ref.ocov_ref
  255.9 7.5 %synthesis_fields.3 = f32[16,48,128]{2,1,0:T(8,128)S(1)} custom-call(s32[1]{0:T(128)} %bitcast.1.core_ref, f32[48,8,768]{2,1,0:T(8,128)S(1)} %bitcast.63, f32[48,8,768]{2,1,0:T(8,128)S(1)} %collective-permute-done.8.other_ref.ocov_ref, f32[8,768]{1,0:T(8,128)S(1)} %copy-done.5, f32[1,128]{1,0:T(1,128)S(1)} %reshape.547.w_ref, ...), custom_call_target="tpu_custom_call" | custom-call | flops 301989888 | bytes 11796480 | tf_op jit(solution)/shard_map/synthesis_fields/pallas_call | solution.py:226
  263.5 13.6 %all_to_all.66.z_ref = f32[16,48,128]{2,1,0:T(8,128)S(1)} all-to-all(f32[16,48,128]{2,1,0:T(8,128)S(1)} %synthesis_fields.3), channel_id=1, replica_groups=mesh['lat'=8,'ord'=16] {'ord'}, dimensions={0} | all-to-all | bytes 786432 | tf_op jit(solution)/shard_map/all_to_all | solution.py:509
  277.1 8.1 %longitude_third.1 = f32[16,2,48,128]{3,2,1,0:T(8,128)S(1)} custom-call(f32[16,48,128]{2,1,0:T(8,128)S(1)} %all_to_all.66.z_ref, f32[768,128]{1,0:T(8,128)S(1)} %broadcast_select_fusion.1.eta_ref, f32[2,768,128]{2,1,0:T(8,128)S(1)} %get-tuple-element.45.first_ref, f32[2,768,128]{2,1,0:T(8,128)S(1)} %get-tuple-element.46.ratio_ref, ...), custom_call_target="tpu_custom_call" | custom-call | flops 2717908992 | bytes 10616832 | tf_op jit(solution)/shard_map/longitude_third/pallas_call | solution.py:444
  285.2 16.8 %all_to_all.67.x_ref = f32[16,2,48,128]{3,2,1,0:T(8,128)S(1)} all-to-all(f32[16,2,48,128]{3,2,1,0:T(8,128)S(1)} %longitude_third.1), channel_id=1, replica_groups=mesh['lat'=8,'ord'=16] {'ord'}, dimensions={0} | all-to-all | bytes 1572864 | tf_op jit(solution)/shard_map/all_to_all | solution.py:509
  302.0 6.4 %analysis_sum.1 = f32[2,48,768]{2,1,0:T(8,128)S(1)} custom-call(f32[16,2,48,128]{3,2,1,0:T(8,128)S(1)} %all_to_all.67.x_ref, f32[2,8,768]{2,1,0:T(8,128)S(1)} %copy-done.3, bf16[48,128,768]{2,1,0:T(8,128)(2,1)} %bitcast.72), custom_call_target="tpu_custom_call" | custom-call | flops 603979776 | bytes 14155776 | tf_op jit(solution)/shard_map/analysis_sum/pallas_call | solution.py:198
  308.5 1.4 collective-permute-done.9
  310.5 2.7 collective-permute-start.11
  313.1 7.0 %collective-permute-done.10 = f32[48,768]{1,0:T(8,128)S(1)} collective-permute-done((f32[48,768]{1,0:T(8,128)S(1)}, f32[48,768]{1,0:T(8,128)S(1)}, u32[]{:S(2)}, u32[]{:S(2)}) %collective-permute-start.10) | collective-permute-done | bytes 147488 | tf_op jit(solution)/shard_map/ppermute | solution.py:528
  321.7 6.6 %synthesis_last.1 = f32[2,48,128]{2,1,0:T(8,128)S(1)} custom-call(s32[1]{0:T(128)} %bitcast.1.core_ref, f32[48,768]{1,0:T(8,128)S(1)} %add_add_fusion.mine_ref, f32[48,768]{1,0:T(8,128)S(1)} %collective-permute-done.13.other_ref, f32[1,128]{1,0:T(1,128)S(1)} %reshape.547.w_ref, bf16[48,128,768]{2,1,0:T(8,128)(2,1)} %bitcast.73), custom_call_target="tpu_custom_call" | custom-call | flops 37748736 | bytes 9732096 | tf_op jit(solution)/shard_map/synthesis_last/pallas_call | solution.py:239
  329.2 3.6 %all-to-all-start.11 = ((f32[16,96,128]{2,1,0:T(8,128)}), f32[16,96,128]{2,1,0:T(8,128)S(1)}, u32[]{:S(2)}, u32[]{:S(2)}) async-start(f32[16,96,128]{2,1,0:T(8,128)} %broadcast_in_dim.233), calls=%async_computation.11 | async-start | bytes 1572864 | tf_op jit(solution)/shard_map/all_to_all | solution.py:509
  332.9 1.8 cosine_multiply_fusion
  334.7 13.3 %all-to-all-done.11 = f32[16,96,128]{2,1,0:T(8,128)S(1)} async-done(((f32[16,96,128]{2,1,0:T(8,128)}), f32[16,96,128]{2,1,0:T(8,128)S(1)}, u32[]{:S(2)}, u32[]{:S(2)}) %all-to-all-start.11) | async-done | bytes 786464 | tf_op jit(solution)/shard_map/all_to_all | solution.py:509
  348.0 1.4 fusion.4
  (130 shorter events, 21.8 us)
Async XLA Ops:
  0.0 9.2 %copy-start.10 = (s32[720]{0:T(1024)S(1)}, s32[720]{0:T(1024)}, u32[]{:S(2)}) copy-start(s32[720]{0:T(1024)} %param.11) | copy-start | bytes 8644
  0.0 12.7 %copy-start.16 = (f32[96]{0:T(128)S(1)}, f32[96]{0:T(128)}, u32[]{:S(2)}) copy-start(f32[96]{0:T(128)} %param.10) | copy-start | bytes 1156
  0.0 13.5 %copy-start.11 = (s32[2,2]{1,0:T(2,128)S(1)}, s32[2,2]{1,0:T(2,128)}, u32[]{:S(2)}) copy-start(s32[2,2]{1,0:T(2,128)} %param.14) | copy-start | bytes 52
  2.1 34.5 %all-to-all-start = ((f32[16,96,128]{2,1,0:T(8,128)}), f32[16,96,128]{2,1,0:T(8,128)S(1)}, u32[]{:S(2)}, u32[]{:S(2)}) async-start(f32[16,96,128]{2,1,0:T(8,128)} %broadcast_in_dim.207), calls=%async_computation | async-start | bytes 1572864 | tf_op jit(solution)/shard_map/all_to_all | solution.py:509
  9.2 2.7 copy-start.13
  9.3 2.6 copy-start.7
  12.8 0.6 copy-start.12
  37.2 13.5 %copy-start.9 = (f32[8,720]{1,0:T(8,128)S(1)}, f32[8,720]{1,0:T(8,128)}, u32[]{:S(2)}) copy-start(f32[8,720]{1,0:T(8,128)} %param.12) | copy-start | bytes 69124
  43.3 1.5 collective-permute-start
  44.7 8.3 %collective-permute-start.1 = (f32[48,768]{1,0:T(8,128)S(1)}, f32[48,768]{1,0:T(8,128)S(1)}, u32[]{:S(2)}, u32[]{:S(2)}) collective-permute-start(f32[48,768]{1,0:T(8,128)S(1)} %bitcast_add_fusion.3), channel_id=1, source_target_pairs={{0,32},{16,48},{32,64},{48,80},{64,96},{80,112},{96,0},{112,16},{1... | collective-permute-start | bytes 442376 | tf_op jit(solution)/shard_map/ppermute | solution.py:528
  46.7 8.8 %collective-permute-start.2 = (f32[48,768]{1,0:T(8,128)S(1)}, f32[48,768]{1,0:T(8,128)S(1)}, u32[]{:S(2)}, u32[]{:S(2)}) collective-permute-start(f32[48,768]{1,0:T(8,128)S(1)} %bitcast_add_fusion.3), channel_id=1, source_target_pairs={{0,96},{16,112},{32,0},{48,16},{64,32},{80,48},{96,64},{112,80},{1... | collective-permute-start | bytes 442376 | tf_op jit(solution)/shard_map/ppermute | solution.py:528
  48.9 8.4 %collective-permute-start.3 = (f32[48,768]{1,0:T(8,128)S(1)}, f32[48,768]{1,0:T(8,128)S(1)}, u32[]{:S(2)}, u32[]{:S(2)}) collective-permute-start(f32[48,768]{1,0:T(8,128)S(1)} %bitcast_add_fusion.3), channel_id=1, source_target_pairs={{0,64},{16,80},{32,96},{48,112},{64,0},{80,16},{96,32},{112,48},{1... | collective-permute-start | bytes 442376 | tf_op jit(solution)/shard_map/ppermute | solution.py:528
  57.4 1.6 collective-permute-start.4
  57.7 9.5 %copy-start.6 = (f32[2,4,768]{2,1,0:T(4,128)}, f32[2,4,768]{2,1,0:T(4,128)S(1)}, u32[]{:S(2)}) copy-start(f32[2,4,768]{2,1,0:T(4,128)S(1)} %broadcast_in_dim.211) | copy-start | bytes 73732
  57.7 9.5 %copy-start.2 = (f32[2,8,768]{2,1,0:T(8,128)}, f32[2,8,768]{2,1,0:T(8,128)S(1)}, u32[]{:S(2)}) copy-start(f32[2,8,768]{2,1,0:T(8,128)S(1)} %constant_dynamic-update-slice_fusion.kap_ref) | copy-start | bytes 147460
  67.2 22.1 %all-to-all-start.1 = ((f32[16,2,48,128]{3,2,1,0:T(8,128)}), f32[16,2,48,128]{3,2,1,0:T(8,128)S(1)}, u32[]{:S(2)}, u32[]{:S(2)}) async-start(f32[16,2,48,128]{3,2,1,0:T(8,128)} %synthesis_first.1), calls=%async_computation.1 | async-start | bytes 1572864 | tf_op jit(solution)/shard_map/all_to_all | solution.py:509
  97.1 0.9 copy-start
  116.6 2.9 collective-permute-start.5
  139.4 19.6 %copy-start.15 = (f32[2,4]{1,0:T(2,128)S(1)}, f32[2,4]{1,0:T(2,128)}, u32[]{:S(2)}) copy-start(f32[2,4]{1,0:T(2,128)} %param.15) | copy-start | bytes 100
  157.6 2.8 collective-permute-start.6
  160.5 0.7 copy-start.4
  169.2 13.9 %all-to-all-start.5 = ((f32[16,48,128]{2,1,0:T(8,128)}), f32[16,48,128]{2,1,0:T(8,128)S(1)}, u32[]{:S(2)}, u32[]{:S(2)}) async-start(f32[16,48,128]{2,1,0:T(8,128)} %synthesis_fields.2), calls=%async_computation.5 | async-start | bytes 786432 | tf_op jit(solution)/shard_map/all_to_all | solution.py:509
  183.2 1.1 copy-start.1
  211.7 2.9 collective-permute-start.7
  234.2 21.7 %copy-start.5 = (f32[8,768]{1,0:T(8,128)S(1)}, f32[8,768]{1,0:T(8,128)}, u32[]{:S(2)}) copy-start(f32[8,768]{1,0:T(8,128)} %squeeze_stack_reshape.3.kap_ref) | copy-start | bytes 73732
  253.1 2.8 collective-permute-start.8
  277.1 24.9 %copy-start.3 = (f32[2,8,768]{2,1,0:T(8,128)S(1)}, f32[2,8,768]{2,1,0:T(8,128)}, u32[]{:S(2)}) copy-start(f32[2,8,768]{2,1,0:T(8,128)} %copy-done.2) | copy-start | bytes 147460
  308.4 1.5 collective-permute-start.9
  309.8 10.3 %collective-permute-start.10 = (f32[48,768]{1,0:T(8,128)S(1)}, f32[48,768]{1,0:T(8,128)S(1)}, u32[]{:S(2)}, u32[]{:S(2)}) collective-permute-start(f32[48,768]{1,0:T(8,128)S(1)} %bitcast_add_fusion.2), channel_id=1, source_target_pairs={{0,32},{16,48},{32,64},{48,80},{64,96},{80,112},{96,0},{112,16},{1... | collective-permute-start | bytes 442376 | tf_op jit(solution)/shard_map/ppermute | solution.py:528
  310.5 9.7 %collective-permute-start.11 = (f32[48,768]{1,0:T(8,128)S(1)}, f32[48,768]{1,0:T(8,128)S(1)}, u32[]{:S(2)}, u32[]{:S(2)}) collective-permute-start(f32[48,768]{1,0:T(8,128)S(1)} %bitcast_add_fusion.2), channel_id=1, source_target_pairs={{0,96},{16,112},{32,0},{48,16},{64,32},{80,48},{96,64},{112,80},{1... | collective-permute-start | bytes 442376 | tf_op jit(solution)/shard_map/ppermute | solution.py:528
  313.1 7.0 %collective-permute-start.12 = (f32[48,768]{1,0:T(8,128)S(1)}, f32[48,768]{1,0:T(8,128)S(1)}, u32[]{:S(2)}, u32[]{:S(2)}) collective-permute-start(f32[48,768]{1,0:T(8,128)S(1)} %bitcast_add_fusion.2), channel_id=1, source_target_pairs={{0,64},{16,80},{32,96},{48,112},{64,0},{80,16},{96,32},{112,48},{1... | collective-permute-start | bytes 442376 | tf_op jit(solution)/shard_map/ppermute | solution.py:528
  320.2 1.5 collective-permute-start.13
  328.2 4.6 %copy-start.8 = (s32[16,48]{1,0:T(8,128)S(1)}, s32[16,48]{1,0:T(8,128)}, u32[]{:S(2)}) copy-start(s32[16,48]{1,0:T(8,128)} %copy-done.7) | copy-start | bytes 9220
  328.3 4.6 %copy-start.14 = (f32[48]{0:T(128)S(1)}, f32[48]{0:T(128)}, u32[]{:S(2)}) copy-start(f32[48]{0:T(128)} %copy-done.13) | copy-start | bytes 580
  329.2 18.8 %all-to-all-start.11 = ((f32[16,96,128]{2,1,0:T(8,128)}), f32[16,96,128]{2,1,0:T(8,128)S(1)}, u32[]{:S(2)}, u32[]{:S(2)}) async-start(f32[16,96,128]{2,1,0:T(8,128)} %broadcast_in_dim.233), calls=%async_computation.11 | async-start | bytes 1572864 | tf_op jit(solution)/shard_map/all_to_all | solution.py:509
